TPU v7x, 128 devices: a whole 4x4x4 slice. The times are simulated.
128 devices in a mesh: tile: 4 (over x), tm: 16 (over y, z), mode: 2 (over core).
Axes of the slice: x: 4, y: 4, z: 4, core: 2. Of those that a mesh axis runs over, the one named last changes fastest.
Arguments:
- object_field: float32 [2, 1056, 4096], P(None, 'tile', 'tm'), may hold values from -4 to 4
- probe_modes: float32 [4, 2, 256, 256], P('mode'), may hold values from -3 to 3
- amplitudes: float32 [128, 256, 256], P(('tile', 'tm')), may hold values from 0.3 to 2.5
- anchors: int32 [128, 1], P(('tile', 'tm')), may hold values from 0 to 14, as said below
- row_offset: int32 [128], P(('tile', 'tm')), may hold values from 0 to 8
- col_offset: int32 [128], P(('tile', 'tm')), may hold values from 0 to 255
- live_counts: int32 [64], P(('tile', 'tm')), may hold values from 1 to 2, as said below
Outputs:
- object_out: float32 [2, 1056, 4096], P(None, 'tile', 'tm')
- probe_out: float32 [4, 2, 256, 256], P('mode')
Inputs may be any that keep to these rules, and one draw needn't show every extreme that they name: The first position of group d has anchor min((d % 16 + 16 // 2) % 16, 14); the other positions' anchors may be any tile of the band up to 14. `live_counts`: some group has all 2 positions live.
All inputs are finite; a program needn't handle non-finite values.
Results may differ from a plain program's by a relative error of at most 0.0033.
Values may be sent and summed in bfloat16 or wider, within the bound.
No kernel may reach another device: no remote copies, remote signals or barrier semaphores. Data moves between devices by JAX's collectives and lax.ppermute only.
A program may use at most 128 MiB of HBM per device.

v0:
```python
import jax
import jax.numpy as jnp
from jax import lax
from jax.sharding import PartitionSpec as P

ITERS = 2


HIGHEST_PREC = lax.Precision.HIGHEST
FLOOR_VALUE = 0.5
OBJECT_REG = 1.0
PROBE_REG = 1.0


def dft_tables(length):
    counter = jnp.arange(length, dtype=jnp.int32)
    phases = counter[:, None] * counter[None, :] % length
    angles = phases.astype(jnp.float32) * (2.0 * jnp.pi / length)
    scaling = 1.0 / jnp.sqrt(jnp.float32(length))
    return (jnp.cos(angles) * scaling, -jnp.sin(angles) * scaling)


def left_product(tables, real_part, imag_part):
    mat_re, mat_im, mat_sum = tables
    first = jnp.einsum("kn,...nm->...km", mat_re, real_part, precision=HIGHEST_PREC)
    second = jnp.einsum("kn,...nm->...km", mat_im, imag_part, precision=HIGHEST_PREC)
    third = jnp.einsum("kn,...nm->...km", mat_sum, real_part + imag_part, precision=HIGHEST_PREC)
    return (first - second, third - first - second)


def right_product(real_part, imag_part, tables):
    mat_re, mat_im, mat_sum = tables
    first = jnp.einsum("...nm,mk->...nk", real_part, mat_re, precision=HIGHEST_PREC)
    second = jnp.einsum("...nm,mk->...nk", imag_part, mat_im, precision=HIGHEST_PREC)
    third = jnp.einsum("...nm,mk->...nk", real_part + imag_part, mat_sum, precision=HIGHEST_PREC)
    return (first - second, third - first - second)


def transform(real_part, imag_part, tables):
    half_re, half_im = left_product(tables, real_part, imag_part)
    return right_product(half_re, half_im, tables)


def exit_waves(patches, probe_modes, amplitudes, live, forward, backward):
    obj_re = patches[:, 0][:, None]
    obj_im = patches[:, 1][:, None]
    probe_re = probe_modes[:, 0][None]
    probe_im = probe_modes[:, 1][None]
    wave_re = probe_re * obj_re - probe_im * obj_im
    wave_im = probe_re * obj_im + probe_im * obj_re
    far_re, far_im = transform(wave_re, wave_im, forward)
    partial_value = jnp.sum(far_re * far_re + far_im * far_im, axis=1).astype(jnp.bfloat16)
    intensity = lax.psum(partial_value, "mode").astype(jnp.float32)
    factor = (amplitudes / jnp.sqrt(jnp.maximum(intensity, FLOOR_VALUE)))[:, None]
    back_re, back_im = transform(far_re * factor, far_im * factor, backward)
    weights = live[:, None, None, None]
    delta_re = (back_re - wave_re) * weights
    delta_im = (back_im - wave_im) * weights
    numerators = jnp.stack(
        [
            jnp.sum(probe_re * delta_re + probe_im * delta_im, axis=1),
            jnp.sum(probe_re * delta_im - probe_im * delta_re, axis=1),
        ],
        axis=1,
    ).astype(jnp.bfloat16)
    probe_term_re = jnp.sum(obj_re * delta_re + obj_im * delta_im, axis=0)
    probe_term_im = jnp.sum(obj_re * delta_im - obj_im * delta_re, axis=0)
    probe_weight = jnp.sum(
        live[:, None, None] * (patches[:, 0] * patches[:, 0] + patches[:, 1] * patches[:, 1]),
        axis=0,
    )
    summed = lax.psum((probe_term_re, probe_term_im, probe_weight), ("tile", "tm"))
    new_probe = probe_modes + jnp.stack([summed[0], summed[1]], axis=1) / (summed[2] + PROBE_REG)
    return (numerators, new_probe)


def update_object(object_field, partial_value):
    totals = lax.psum(partial_value, "mode")
    return object_field + totals[:2] / (totals[2][None] + OBJECT_REG)


def deposit_all(pieces, rows_at, cols_at, shape_out):

    def deposit(slot_id, accumulator):
        piece = pieces(slot_id)
        region = lax.dynamic_slice(
            accumulator, (0, rows_at[slot_id], cols_at[slot_id]), piece.shape
        )
        return lax.dynamic_update_slice(
            accumulator, region + piece, (0, rows_at[slot_id], cols_at[slot_id])
        )

    return lax.fori_loop(0, rows_at.shape[0], deposit, jnp.zeros(shape_out, jnp.float32))


def body(object_field, probe_modes, amplitudes, anchors, row_offset, col_offset, live_counts):
    tile_rows = object_field.shape[1]
    tile_cols = object_field.shape[2]
    patch_len = probe_modes.shape[-1]
    per_device = amplitudes.shape[0]
    tm_size = lax.axis_size("tm")
    mat_re, mat_im = dft_tables(patch_len)
    forward = (mat_re, mat_im, mat_re + mat_im)
    backward = (mat_re, -mat_im, mat_re - mat_im)
    slot_ids = jnp.arange(per_device, dtype=jnp.int32)
    live = (slot_ids < live_counts[0]).astype(jnp.float32)
    anchor_ids = anchors[:, 0]
    starts = anchor_ids * tile_cols + col_offset
    for iteration in range(ITERS):
        low_tile = object_field.astype(jnp.bfloat16)
        band_tile = lax.all_gather(low_tile, "tm", axis=2, tiled=True)
        source = band_tile

        def cut_window(row_at, col_at):
            return lax.dynamic_slice(source, (0, row_at, col_at), (2, patch_len, patch_len))

        patches = jax.vmap(cut_window)(row_offset, starts).astype(jnp.float32)
        numerators, new_probe = exit_waves(
            patches, probe_modes, amplitudes, live, forward, backward
        )
        probe_power = jnp.sum(
            probe_modes[:, 0] * probe_modes[:, 0] + probe_modes[:, 1] * probe_modes[:, 1], axis=0
        )

        def band_piece(slot_id):
            return jnp.concatenate(
                [numerators[slot_id].astype(jnp.float32), (probe_power * live[slot_id])[None]],
                axis=0,
            )

        accumulator = deposit_all(
            band_piece, row_offset, starts, (3, tile_rows, tm_size * tile_cols)
        )
        own_part = lax.psum_scatter(accumulator, "tm", scatter_dimension=2, tiled=True)
        object_field = update_object(object_field, own_part)
        probe_modes = new_probe
    return (object_field, probe_modes)


def solution(mesh):
    placed = (
        P(None, "tile", "tm"),
        P("mode", None, None, None),
        P(("tile", "tm"), None, None),
        P(("tile", "tm"), None),
        P(("tile", "tm")),
        P(("tile", "tm")),
        P(("tile", "tm")),
    )
    return jax.shard_map(
        body,
        mesh=mesh,
        in_specs=placed,
        out_specs=(P(None, "tile", "tm"), P("mode", None, None, None)),
        check_vma=False,
    )
```

profile of v0, /device:TPU:1, one launch (start us, length us, event | category | flops | bytes accessed | tf_op | source)
XLA Modules:
  0.0 892.6 jit_solution(14328135099886391233)
XLA Ops:
  11.9 59.5 %all-gather.3.cloned.1.call-done = bf16[2,264,4096]{2,1,0:T(8,128)(2,1)} async-done(((bf16[2,264,256]{2,1,0:T(8,128)(2,1)}), bf16[2,264,4096]{2,1,0:T(8,128)(2,1)}) %all-gather.3.cloned.1.call-update) | async-done | bytes 4325392 | tf_op jit(solution)/shard_map/all_gather | solution.py:111
  71.4 6.2 while.30
  93.0 5.1 add_reduce_fusion.5
  98.9 23.7 %all-reduce.9.cloned.1.call-done = bf16[2,256,256]{2,1,0:T(8,128)(2,1)} async-done(((bf16[2,256,256]{2,1,0:T(8,128)(2,1)}), bf16[2,256,256]{2,1,0:T(8,128)(2,1)}) %all-reduce.9.cloned.1.call-update) | async-done | bytes 262160 | tf_op jit(solution)/shard_map/psum | solution.py:53
  142.0 4.8 add_reduce_fusion.3
  146.8 6.3 broadcast.72.clone
  153.1 33.5 %while.28 = (s32[]{:T(128)}, f32[3,264,4096]{2,1,0:T(8,128)}, s32[2]{0:T(128)S(1)}, s32[2]{0:T(128)S(1)}, bf16[2,2,256,256]{3,2,1,0:T(8,128)(2,1)S(1)}, /*index=...) while((s32[]{:T(128)}, f32[3,264,4096]{2,1,0:T(8,128)}, ...), condition=%wide.region_6.7_spmd, body=%wide.region_5.6_spmd.sunk | while | flops 589832 | bytes 5243113 | solution.py:93
  161.1 8.8 dynamic_update_slice.16
  177.8 8.8 dynamic_update_slice.16
  186.7 96.9 %reduce-scatter.3.cloned.1.call-done = f32[3,264,256]{2,1,0:T(8,128)} async-done(((f32[3,264,4096]{2,1,0:T(8,128)}), f32[3,264,256]{2,1,0:T(8,128)}) %reduce-scatter.3.cloned.1.call-update) | async-done | bytes 811024 | tf_op jit(solution)/shard_map/reduce_scatter | solution.py:134
  283.6 26.6 %all-reduce.11.cloned.1.call-done = f32[3,264,256]{2,1,0:T(8,128)} async-done(((f32[3,264,256]{2,1,0:T(8,128)}), f32[3,264,256]{2,1,0:T(8,128)}) %all-reduce.11.cloned.1.call-update) | async-done | bytes 811024 | tf_op jit(solution)/shard_map/psum | solution.py:78
  313.8 58.5 %all-gather.5.cloned.1.call-done = bf16[2,264,4096]{2,1,0:T(8,128)(2,1)} async-done(((bf16[2,264,256]{2,1,0:T(8,128)(2,1)}), bf16[2,264,4096]{2,1,0:T(8,128)(2,1)}) %all-gather.5.cloned.1.call-update) | async-done | bytes 4325392 | tf_op jit(solution)/shard_map/all_gather | solution.py:111
  372.3 6.4 while.31
  382.2 130.1 %all-reduce.19.cloned.1.call-done = (f32[2,1,256,256]{3,2,1,0:T(8,128)}, f32[2,1,256,256]{3,2,1,0:T(8,128)}, f32[256,256]{1,0:T(8,128)}) async-done(((f32[2,1,256,256]{3,2,1,0:T(8,128)}, f32[2,1,256,256]{3,2,1,0:T(8,128)}, f32[256,256]{1,0:T(8,128)}), (f32[2,1,256,256]{3,2,1,0:T(8,128)}, f32[2,1,256,256]{3,2,1,0:T(8,128)}, f32[256,256]{1,0:T(8,128)})) %all-reduce.19.cloned.1.call-update) | async-done | bytes 1310736 | tf_op jit(solution)/shard_map/psum | solution.py:72
  529.9 5.1 add_reduce_fusion.2
  536.4 22.1 %all-reduce.13.cloned.1.call-done = bf16[2,256,256]{2,1,0:T(8,128)(2,1)} async-done(((bf16[2,256,256]{2,1,0:T(8,128)(2,1)}), bf16[2,256,256]{2,1,0:T(8,128)(2,1)}) %all-reduce.13.cloned.1.call-update) | async-done | bytes 262160 | tf_op jit(solution)/shard_map/psum | solution.py:53
  577.8 4.8 add_reduce_fusion
  582.7 6.3 broadcast.72
  589.0 33.5 %while.29 = (s32[]{:T(128)}, f32[3,264,4096]{2,1,0:T(8,128)}, s32[2]{0:T(128)S(1)}, s32[2]{0:T(128)S(1)}, bf16[2,2,256,256]{3,2,1,0:T(8,128)(2,1)S(1)}, /*index=...) while((s32[]{:T(128)}, f32[3,264,4096]{2,1,0:T(8,128)}, ...), condition=%wide.region_21.22_spmd, body=%wide.region_20.21_spmd.sunk | while | flops 589832 | bytes 5243113 | solution.py:93
  596.9 8.8 dynamic_update_slice.17
  613.7 8.8 dynamic_update_slice.17
  623.3 96.3 %reduce-scatter.5.cloned.1.call-done = f32[3,264,256]{2,1,0:T(8,128)} async-done(((f32[3,264,4096]{2,1,0:T(8,128)}), f32[3,264,256]{2,1,0:T(8,128)}) %reduce-scatter.5.cloned.1.call-update) | async-done | bytes 811024 | tf_op jit(solution)/shard_map/reduce_scatter | solution.py:134
  719.6 136.1 %all-reduce.17.cloned.1.call-done = (f32[2,1,256,256]{3,2,1,0:T(8,128)}, f32[2,1,256,256]{3,2,1,0:T(8,128)}, f32[256,256]{1,0:T(8,128)}) async-done(((f32[2,1,256,256]{3,2,1,0:T(8,128)}, f32[2,1,256,256]{3,2,1,0:T(8,128)}, f32[256,256]{1,0:T(8,128)}), (f32[2,1,256,256]{3,2,1,0:T(8,128)}, f32[2,1,256,256]{3,2,1,0:T(8,128)}, f32[256,256]{1,0:T(8,128)})) %all-reduce.17.cloned.1.call-update) | async-done | bytes 1310736 | tf_op jit(solution)/shard_map/psum | solution.py:72
  859.3 23.0 %all-reduce.15.cloned.1.call-done = f32[3,264,256]{2,1,0:T(8,128)} async-done(((f32[3,264,256]{2,1,0:T(8,128)}), f32[3,264,256]{2,1,0:T(8,128)}) %all-reduce.15.cloned.1.call-update) | async-done | bytes 811024 | tf_op jit(solution)/shard_map/psum | solution.py:78
  (134 shorter events, 121.3 us)
Async XLA Ops:
  7.2 64.2 %all-gather.3.cloned.1.call-start = ((), (), s32[]{:S(2)}) async-start(), calls=%async_computation.2 | async-start | bytes 4595712 | tf_op jit(solution)/shard_map/all_gather | solution.py:111
  9.0 113.6 %all-reduce.9.cloned.1.call-start = ((), (), s32[]{:S(2)}) async-start(), calls=%async_computation.3 | async-start | bytes 524288 | tf_op jit(solution)/shard_map/psum | solution.py:53
  77.7 1.0 copy-start.2
  77.7 21.1 %copy-start = (f32[2,2,256,256]{3,2,1,0:T(8,128)S(1)}, f32[2,2,256,256]{3,2,1,0:T(8,128)}, u32[]{:S(2)}) copy-start(f32[2,2,256,256]{3,2,1,0:T(8,128)} %param.12) | copy-start | bytes 3145732
  98.1 185.5 %reduce-scatter.3.cloned.1.call-start = ((), (), s32[]{:S(2)}) async-start(), calls=%async_computation.4 | async-start | bytes 13787136 | tf_op jit(solution)/shard_map/reduce_scatter | solution.py:134
  142.0 11.2 %copy-start.13 = (s32[2]{0:T(128)S(1)}, s32[2]{0:T(128)}, u32[]{:S(2)}) copy-start(s32[2]{0:T(128)} %param.15) | copy-start | bytes 28
  186.6 125.3 %copy-start.4 = (f32[2,264,256]{2,1,0:T(8,128)S(1)}, f32[2,264,256]{2,1,0:T(8,128)}, u32[]{:S(2)}) copy-start(f32[2,264,256]{2,1,0:T(8,128)} %param.11) | copy-start | bytes 1622020
  186.6 194.0 %copy-start.3 = (f32[2,2,256,256]{3,2,0,1:T(8,128)S(1)}, f32[2,2,256,256]{3,2,0,1:T(8,128)}, u32[]{:S(2)}) copy-start(f32[2,2,256,256]{3,2,0,1:T(8,128)} %copy-done.2) | copy-start | bytes 3145732
  186.7 123.6 %all-reduce.11.cloned.1.call-start = ((), (), s32[]{:S(2)}) async-start(), calls=%async_computation.5 | async-start | bytes 1622016 | tf_op jit(solution)/shard_map/psum | solution.py:78
  283.6 88.7 %all-gather.5.cloned.1.call-start = ((), (), s32[]{:S(2)}) async-start(), calls=%async_computation.6 | async-start | bytes 4595712 | tf_op jit(solution)/shard_map/all_gather | solution.py:111
  311.2 0.7 copy-start.6
  313.7 198.6 %all-reduce.19.cloned.1.call-start = ((), (), s32[]{:S(2)}) async-start(), calls=%async_computation.11 | async-start | bytes 2621440 | tf_op jit(solution)/shard_map/psum | solution.py:72
  378.7 0.8 copy-start.12
  381.7 176.8 %all-reduce.13.cloned.1.call-start = ((), (), s32[]{:S(2)}) async-start(), calls=%async_computation.7 | async-start | bytes 524288 | tf_op jit(solution)/shard_map/psum | solution.py:53
  513.3 5.2 copy-start.8
  514.8 1.0 copy-start.1
  535.0 184.5 %reduce-scatter.5.cloned.1.call-start = ((), (), s32[]{:S(2)}) async-start(), calls=%async_computation.8 | async-start | bytes 13787136 | tf_op jit(solution)/shard_map/reduce_scatter | solution.py:134
  622.4 234.2 %copy-start.9 = (f32[256,256]{1,0:T(8,128)S(1)}, f32[256,256]{1,0:T(8,128)}, u32[]{:S(2)}) copy-start(f32[256,256]{1,0:T(8,128)} %copy-done.8) | copy-start | bytes 786436
  622.4 234.2 %copy-start.11 = (f32[2,1,256,256]{3,2,1,0:T(8,128)S(1)}, f32[2,1,256,256]{3,2,1,0:T(8,128)}, u32[]{:S(2)}) copy-start(f32[2,1,256,256]{3,2,1,0:T(8,128)} %get-tuple-element.337) | copy-start | bytes 1572868
  622.4 260.9 %copy-start.5 = (f32[2,264,256]{2,1,0:T(8,128)S(1)}, f32[2,264,256]{2,1,0:T(8,128)}, u32[]{:S(2)}) copy-start(f32[2,264,256]{2,1,0:T(8,128)} %param.11) | copy-start | bytes 1622020
  622.5 260.9 %copy-start.7 = (f32[264,256]{1,0:T(8,128)S(1)}, f32[264,256]{1,0:T(8,128)}, u32[]{:S(2)}) copy-start(f32[264,256]{1,0:T(8,128)} %copy-done.6) | copy-start | bytes 811012
  622.5 260.9 %copy-start.10 = (f32[3,264,256]{2,1,0:T(8,128)S(1)}, f32[3,264,256]{2,1,0:T(8,128)}, u32[]{:S(2)}) copy-start(f32[3,264,256]{2,1,0:T(8,128)} %all-reduce.11.cloned.1.call-done) | copy-start | bytes 2433028
  622.5 233.2 %all-reduce.17.cloned.1.call-start = ((), (), s32[]{:S(2)}) async-start(), calls=%async_computation.10 | async-start | bytes 2621440 | tf_op jit(solution)/shard_map/psum | solution.py:72
  623.2 259.1 %all-reduce.15.cloned.1.call-start = ((), (), s32[]{:S(2)}) async-start(), calls=%async_computation.9 | async-start | bytes 1622016 | tf_op jit(solution)/shard_map/psum | solution.py:78
Sparse Core Ops, SparseCore 0:
  10.7 60.6 all-gather.2
  98.2 24.3 all-reduce.8
  186.8 96.7 reduce-scatter.2
  285.9 24.2 all-reduce.10
  313.9 58.3 all-gather.4
  381.8 130.5 all-reduce.18
  535.1 23.2 all-reduce.12
  622.6 96.8 reduce-scatter.4
  726.3 129.4 all-reduce.16
  858.0 24.3 all-reduce.14
where the time goes:
time: 904 us; the launch traced here: 893 us
  waiting for transfers between devices  674 us (75%)
  matrix products  84.4 us (9%)
  local copies, waits for them, and re-layouts  72.6 us (8%)
  other arithmetic  30.2 us (3%)
  between operations  15.6 us (2%)
  loops' own time  15.4 us (2%)
    psum x2, waiting for transfers between devices, exit_waves(): lax.psum((probe_term_re, probe_term_im, probe_weight), ('tile', 'tm'))  266 us
    reduce_scatter x2, waiting for transfers between devices, body(): lax.psum_scatter(accumulator, 'tm', scatter_dimension=2, tiled=True)  193 us
    all_gather x2, waiting for transfers between devices, body(): band_tile = lax.all_gather(low_tile, 'tm', axis=2, tiled=True)  118 us
    psum x2, waiting for transfers between devices, update_object(): totals = lax.psum(partial_value, 'mode')  49.6 us
    psum x2, waiting for transfers between devices, exit_waves(): intensity = lax.psum(partial_value, 'mode').astype(jnp.float32)  45.8 us
    dynamic_update_slice x4, local copies, waits for them, and re-layouts, deposit(): lax.dynamic_update_slice(accumulator, region + piece, (0, rows_at[slot_id...  35.1 us
    dot_general x4, matrix products, right_product(): jnp.einsum('...nm,mk->...nk', real_part + imag_part, mat_sum, precision=H...  19.7 us
  transfers between devices with their start and end apart: 10, of which 10 were waited for; matrix products, arithmetic and copies ran while one was open for 1% of the time, Pallas kernels for 0%

commit v1 on v0

v1 whole, which is shorter than its diff:
```python
import functools

import jax
import jax.numpy as jnp
import ml_dtypes
import numpy as np
from jax import lax
from jax.experimental import pallas as pl
from jax.experimental.pallas import tpu as pltpu
from jax.sharding import PartitionSpec as P

PS = 256
BH = 264
N_TM = 16
CH = 16
HALO = 24
FLOOR_VALUE = 0.5
OBJECT_REG = 1.0
PROBE_REG = 1.0
F32 = jnp.float32
BF16 = jnp.bfloat16
SWAP = [(0, 1), (1, 0)]

VM = pl.BlockSpec(memory_space=pltpu.VMEM)
SM = pl.BlockSpec(memory_space=pltpu.SMEM)


def dft_tables():
    k = np.arange(PS)
    angle = (k[:, None] * k[None, :] % PS) * (2.0 * np.pi / PS)
    re, im = np.cos(angle) / np.sqrt(PS), -np.sin(angle) / np.sqrt(PS)
    fwd = np.block([[re, -im], [im, re]]).astype(np.float32)
    bwd = np.block([[re, im], [-im, re]]).astype(np.float32)
    out = []
    for table in (fwd, bwd):
        high = table.astype(ml_dtypes.bfloat16)
        low = (table - high.astype(np.float32)).astype(ml_dtypes.bfloat16)
        out += [high, low]
    return out


def call(kernel, out_shape, in_specs, scratch=(), flops=0, nbytes=1 << 20):
    many = isinstance(out_shape, (tuple, list))
    return pl.pallas_call(
        kernel,
        out_shape=out_shape,
        in_specs=in_specs,
        out_specs=[VM] * len(out_shape) if many else VM,
        scratch_shapes=list(scratch),
        compiler_params=pltpu.CompilerParams(vmem_limit_bytes=48 << 20),
        cost_estimate=pl.CostEstimate(flops=flops, bytes_accessed=nbytes, transcendentals=0),
    )


def arr(shape, dtype):
    return jax.ShapeDtypeStruct(shape, dtype)


def lanes(rows):
    return lax.broadcasted_iota(jnp.int32, (rows, PS), 1)


def prep_kernel(idx, anchors, row_offset, col_offset, live_counts, obj, out):
    core = idx[0]
    lane = lanes(8)
    meta = jnp.zeros((8, PS), F32)
    for p in range(2):
        alive = jnp.where(p < live_counts[0], 1, 0)
        for k, value in enumerate((anchors[p, 0], col_offset[p], row_offset[p], alive)):
            meta = jnp.where(lane == 4 * p + k, value.astype(F32), meta)
    for i in range(N_TM):
        out[i, 0:HALO, :] = obj[core, CH * i : CH * i + HALO, :]
        out[i, HALO : HALO + 8, :] = meta


def cut_windows(meta, load, out):
    def visit(t, carry):
        for p in range(2):
            at, col, row = meta[t, 4 * p], meta[t, 4 * p + 1], meta[t, 4 * p + 2]
            both = jnp.where(lanes(HALO) >= col, load(at), load(at + 1))
            both = pltpu.roll(both, lax.rem(HALO - row, HALO), 0)
            out[t, CH * p : CH * p + CH, :] = both[0:CH].astype(BF16)
        return carry

    lax.fori_loop(0, N_TM, visit, 0)


def window_kernel(meta, obj, out):
    cut_windows(meta, lambda at: obj[at, 0:HALO, :], out)


def shift_rows(block, row):
    return pltpu.roll(block, lax.rem(HALO + row, 32), 0)[0:HALO]


def accumulate(meta, idx, parts, power, num, weight):
    num[...] = jnp.zeros_like(num)
    weight[...] = jnp.zeros_like(weight)
    first = pl.multiple_of(idx[1] * CH, CH)

    def visit(t, carry):
        both = parts[t, 80:128, :].astype(F32)
        for p in range(2):
            at, col, row, alive = (meta[t, 4 * p + k] for k in range(4))
            mask = lanes(HALO) >= col
            piece = both[HALO * p : HALO * p + HALO]
            num[at] += jnp.where(mask, piece, 0.0)
            num[at + 1] += jnp.where(mask, 0.0, piece)
            cover = pltpu.roll(shift_rows(power[pl.ds(first, 32), :], row), col, 1) * alive.astype(F32)
            weight[at] += jnp.where(mask, cover, 0.0)
            weight[at + 1] += jnp.where(mask, 0.0, cover)
        return carry

    lax.fori_loop(0, N_TM, visit, 0)


def update_kernel(meta, idx, parts, power, obj, out, upd, num, weight, fresh):
    accumulate(meta, idx, parts, power, num, weight)

    def visit(t, carry):
        step = num[t] / (weight[t] + OBJECT_REG)
        upd[t] = step
        fresh[t] = obj[t, 0:HALO, :] + step
        return carry

    lax.fori_loop(0, N_TM, visit, 0)
    cut_windows(meta, lambda at: fresh[at], out)


def last_update_kernel(meta, idx, parts, power, upd, out, num, weight):
    accumulate(meta, idx, parts, power, num, weight)

    def visit(t, carry):
        total = upd[t] + num[t] / (weight[t] + OBJECT_REG)
        out[t] = jnp.concatenate([total, jnp.zeros((8, PS), F32)], axis=0).astype(BF16)
        return carry

    lax.fori_loop(0, N_TM, visit, 0)


def probe_sum_kernel(parts, out):
    total = lax.fori_loop(0, N_TM, lambda t, acc: acc + parts[t, 0:80, :].astype(F32), jnp.zeros((80, PS), F32))
    out[...] = total.astype(BF16)


def probe_update_kernel(own, one, two, three, objs, out):
    total = (own[...].astype(F32) + two[...].astype(F32)) + (one[...].astype(F32) + three[...].astype(F32))
    scale = 1.0 / (total[64:80] + PROBE_REG)
    step = (total[0:64] * jnp.concatenate([scale] * 4, axis=0)).astype(BF16)

    def visit(t, carry):
        out[t, 0:32, :] = objs[t]
        out[t, 32:96, :] = step
        return carry

    lax.fori_loop(0, N_TM, visit, 0)


def pack_kernel(idx, keep, recv, out):
    first = idx[0] == 0

    def visit(t, carry):
        mine, theirs = keep[t].astype(F32), recv[t].astype(F32)
        out[t, 0:80, :] = (mine[0:80] + theirs[0:80]).astype(BF16)
        num_mine, num_theirs = mine[80 : 80 + HALO], theirs[80 : 80 + HALO]
        out[t, 80:128, :] = jnp.concatenate(
            [jnp.where(first, num_mine, num_theirs), jnp.where(first, num_theirs, num_mine)], axis=0
        ).astype(BF16)
        return carry

    lax.fori_loop(0, N_TM, visit, 0)


def split(value):
    high = value.astype(BF16)
    return high, (value - high.astype(F32)).astype(BF16)


def dot(a, b):
    return lax.dot_general(a, b, (((1,), (0,)), ((), ())), preferred_element_type=F32)


def position_kernel(
    with_update, idx, row_offset, col_offset, live_counts, mh, ml, nh, nl, p_own, p_oth, h_own, h_oth, amp,
    keep, send, power, obj, probe, far, xh, xl, yh, yl, res, factor, group, num, shifted,
):
    core = idx[0]
    first = core == 0
    col, row = col_offset[core], row_offset[core]
    alive = jnp.where(core < live_counts[0], 1, 0).astype(F32)
    back_col = lax.rem(PS - col, PS)

    def rows_of(i):
        return pl.ds(pl.multiple_of(i * CH, CH), CH)

    power[0:8, :] = jnp.zeros((8, PS), F32)
    power[264:272, :] = jnp.zeros((8, PS), F32)

    def stage(i, carry):
        rows = rows_of(i)
        mine = jnp.where(first, h_own[i, 0:CH, :].astype(F32), h_own[i, CH : 2 * CH, :].astype(F32))
        theirs = jnp.where(first, h_oth[i, 0:CH, :].astype(F32), h_oth[i, CH : 2 * CH, :].astype(F32))
        obj_re = pltpu.roll(jnp.where(first, mine, theirs), back_col, 1)
        obj_im = pltpu.roll(jnp.where(first, theirs, mine), back_col, 1)
        obj[0, rows, :] = obj_re
        obj[1, rows, :] = obj_im
        denom = ((obj_re * obj_re + obj_im * obj_im) * alive).astype(BF16)
        keep[i, 64:80, :] = denom
        send[i, 64:80, :] = denom
        total = jnp.zeros((CH, PS), F32)
        for m in range(4):
            src, chunk = (p_own, h_own) if m < 2 else (p_oth, h_oth)
            for k in range(2):
                value = src[m % 2, k, rows, :]
                if with_update:
                    at = 32 + CH * (2 * (m % 2) + k)
                    value = value + chunk[i, at : at + CH, :].astype(F32)
                probe[m, k, rows, :] = value
                total = total + value * value
        power[pl.ds(pl.multiple_of(i * CH + 8, 8), CH), :] = total
        return carry

    lax.fori_loop(0, N_TM, stage, 0)

    def wave(m, rows):
        pr, pi = probe[m, 0, rows, :], probe[m, 1, rows, :]
        o_r, o_i = obj[0, rows, :], obj[1, rows, :]
        return pr, pi, o_r, o_i, pr * o_r - pi * o_i, pr * o_i + pi * o_r

    def put_x(i, re, im):
        for k, value in enumerate((re, im)):
            rows = pl.ds(pl.multiple_of(i * CH + k * PS, CH), CH)
            xh[rows, :], xl[rows, :] = split(value)

    def transform(left_h, left_l, right_h, right_l, out):
        high, low = xh[...], xl[...]
        half = dot(left_h[...], high) + dot(left_h[...], low) + dot(left_l[...], high)
        for k in range(2):
            yh[:, k * PS : (k + 1) * PS], yl[:, k * PS : (k + 1) * PS] = split(half[k * PS : (k + 1) * PS])
        high, low = yh[...], yl[...]
        out[...] = dot(high, right_h[...]) + dot(low, right_h[...]) + dot(high, right_l[...])

    def forward(m, carry):
        def pre(i, carry):
            values = wave(m, rows_of(i))
            put_x(i, values[4], values[5])
            return carry

        lax.fori_loop(0, N_TM, pre, 0)
        transform(mh, ml, nh, nl, far.at[m])
        return carry

    lax.fori_loop(0, 4, forward, 0)

    def intensity(i, carry):
        rows = rows_of(i)
        total = jnp.zeros((CH, PS), F32)
        for g in range(2):
            part = jnp.zeros((CH, PS), F32)
            for m in (2 * g, 2 * g + 1):
                re, im = far[m, rows, 0:PS], far[m, rows, PS : 2 * PS]
                part = part + (re * re + im * im)
            total = total + part.astype(BF16).astype(F32)
        factor[rows, :] = amp[core, rows, :] * lax.rsqrt(jnp.maximum(total, FLOOR_VALUE))
        return carry

    lax.fori_loop(0, N_TM, intensity, 0)

    for g in range(2):
        target = (keep, send)[g]

        def backward(mm, carry, g=g, target=target):
            m = 2 * g + mm

            def pre(i, carry):
                rows = rows_of(i)
                f = factor[rows, :]
                put_x(i, far[m, rows, 0:PS] * f, far[m, rows, PS : 2 * PS] * f)
                return carry

            lax.fori_loop(0, N_TM, pre, 0)
            transform(nh, nl, mh, ml, res)

            def post(i, carry):
                rows = rows_of(i)
                pr, pi, o_r, o_i, wr, wi = wave(m, rows)
                dr = (res[rows, 0:PS] - wr) * alive
                di = (res[rows, PS : 2 * PS] - wi) * alive
                at = pl.multiple_of(mm * 2 * CH, 2 * CH)
                target[i, pl.ds(at, 2 * CH), :] = jnp.concatenate(
                    [o_r * dr + o_i * di, o_r * di - o_i * dr], axis=0
                ).astype(BF16)
                group[mm, 0, rows, :] = pr * dr + pi * di
                group[mm, 1, rows, :] = pr * di - pi * dr
                return carry

            lax.fori_loop(0, N_TM, post, 0)
            return carry

        lax.fori_loop(0, 2, backward, 0)

        def gather(i, carry, g=g):
            rows = rows_of(i)
            for k in range(2):
                part = (group[0, k, rows, :] + group[1, k, rows, :]).astype(BF16).astype(F32)
                num[k, rows, :] = part if g == 0 else num[k, rows, :] + part
            return carry

        lax.fori_loop(0, N_TM, gather, 0)

    shifted[:, 0:8, :] = jnp.zeros((2, 8, PS), F32)
    shifted[:, 264:272, :] = jnp.zeros((2, 8, PS), F32)

    def place(i, carry):
        for k in range(2):
            shifted[k, pl.ds(pl.multiple_of(i * CH + 8, 8), CH), :] = pltpu.roll(num[k, rows_of(i), :], col, 1)
        return carry

    lax.fori_loop(0, N_TM, place, 0)

    def emit(i, carry):
        rows = pl.ds(pl.multiple_of(i * CH, CH), 32)
        pad = jnp.zeros((8, PS), F32)
        re, im = (
            jnp.concatenate([shift_rows(shifted[k, rows, :], row), pad], axis=0) for k in range(2)
        )
        keep[i, 80:112, :] = jnp.where(first, re, im).astype(BF16)
        send[i, 80:112, :] = jnp.where(first, im, re).astype(BF16)
        return carry

    lax.fori_loop(0, N_TM, emit, 0)


def final_kernel(idx, obj, p_own, h_one, h_own, h_oth, obj_out, probe_out):
    core = idx[0]

    def visit(i, carry):
        rows = pl.ds(pl.multiple_of(i * CH, CH), CH)
        obj_out[core, rows, :] = obj[core, rows, :] + h_own[i, 0:CH, :].astype(F32)
        obj_out[1 - core, rows, :] = obj[1 - core, rows, :] + h_oth[i, 0:CH, :].astype(F32)
        for m in range(2):
            for k in range(2):
                at = 32 + CH * (2 * m + k)
                before = p_own[m, k, rows, :] + h_one[i, at : at + CH, :].astype(F32)
                probe_out[m, k, rows, :] = before + h_own[i, at : at + CH, :].astype(F32)
        return carry

    lax.fori_loop(0, N_TM, visit, 0)
    last = N_TM - 1
    obj_out[core, 256:264, :] = obj[core, 256:264, :] + h_own[last, 16:32, :].astype(F32)[0:8]
    obj_out[1 - core, 256:264, :] = obj[1 - core, 256:264, :] + h_oth[last, 16:32, :].astype(F32)[0:8]


def body(object_field, probe_modes, amplitudes, anchors, row_offset, col_offset, live_counts):
    idx = jnp.stack([lax.axis_index("mode"), lax.axis_index("tm")]).astype(jnp.int32)
    tables = [jnp.asarray(t) for t in dft_tables()]

    def exchange(x):
        return lax.all_to_all(x, "tm", 0, 0)

    def swap(x):
        return lax.ppermute(x, "mode", SWAP)

    def over_tiles(x):
        n = lax.axis_size("tile")
        return [lax.ppermute(x, "tile", [(i, (i + k) % n) for i in range(n)]) for k in (1, 2, 3)]

    probe_other = swap(probe_modes)
    slots = call(prep_kernel, arr((N_TM, 32, PS), F32), [SM] * 5 + [VM])(
        idx, anchors, row_offset, col_offset, live_counts, object_field
    )
    obj = exchange(slots)
    meta = obj[:, HALO, 0:8].astype(jnp.int32)
    windows = call(window_kernel, arr((N_TM, 32, PS), BF16), [SM, VM])(meta, obj)
    h_own = exchange(windows)
    h_first = h_own

    for iteration in range(2):
        h_oth = swap(h_own)
        part = arr((N_TM, 112, PS), BF16)
        keep, send, power = call(
            functools.partial(position_kernel, iteration > 0),
            (part, part, arr((272, PS), F32)),
            [SM] * 4 + [VM] * 9,
            scratch=[
                pltpu.VMEM((2, PS, PS), F32),
                pltpu.VMEM((4, 2, PS, PS), F32),
                pltpu.VMEM((4, PS, 2 * PS), F32),
                pltpu.VMEM((2 * PS, PS), BF16),
                pltpu.VMEM((2 * PS, PS), BF16),
                pltpu.VMEM((PS, 2 * PS), BF16),
                pltpu.VMEM((PS, 2 * PS), BF16),
                pltpu.VMEM((PS, 2 * PS), F32),
                pltpu.VMEM((PS, PS), F32),
                pltpu.VMEM((2, 2, PS, PS), F32),
                pltpu.VMEM((2, PS, PS), F32),
                pltpu.VMEM((2, 272, PS), F32),
            ],
            flops=16 * 3 * 2 * 512 * 512 * 256,
            nbytes=10 << 20,
        )(idx, row_offset, col_offset, live_counts, *tables, probe_modes, probe_other, h_own, h_oth, amplitudes)
        recv = swap(send)
        parts = call(pack_kernel, arr((N_TM, 128, PS), BF16), [SM, VM, VM])(idx, keep, recv)
        parts = exchange(parts)
        probe_part = call(probe_sum_kernel, arr((80, PS), BF16), [VM])(parts)
        others = over_tiles(probe_part)
        chunk = pltpu.VMEM((N_TM, HALO, PS), F32)
        if iteration == 0:
            objs, upd = call(
                update_kernel,
                (arr((N_TM, 32, PS), BF16), arr((N_TM, HALO, PS), F32)),
                [SM, SM, VM, VM, VM],
                scratch=[chunk] * 3,
                nbytes=8 << 20,
            )(meta, idx, parts, power, obj)
        else:
            objs = call(
                last_update_kernel,
                arr((N_TM, 32, PS), BF16),
                [SM, SM, VM, VM, VM],
                scratch=[chunk] * 2,
                nbytes=8 << 20,
            )(meta, idx, parts, power, upd)
        h_first = h_own
        h_own = exchange(
            call(probe_update_kernel, arr((N_TM, 96, PS), BF16), [VM] * 5)(probe_part, *others, objs)
        )

    return call(
        final_kernel, (arr((2, BH, PS), F32), arr((2, 2, PS, PS), F32)), [SM] + [VM] * 5
    )(idx, object_field, probe_modes, h_first, h_own, swap(h_own))


def solution(mesh):
    placed = (
        P(None, "tile", "tm"),
        P("mode", None, None, None),
        P(("tile", "tm"), None, None),
        P(("tile", "tm"), None),
        P(("tile", "tm")),
        P(("tile", "tm")),
        P(("tile", "tm")),
    )
    return jax.shard_map(
        body,
        mesh=mesh,
        in_specs=placed,
        out_specs=(P(None, "tile", "tm"), P("mode", None, None, None)),
        check_vma=False,
    )
```

time: 904 us -> 190 us (0.21); the launches traced: 893 us -> 189 us
  waiting for transfers between devices: 674 us -> 20.7 us
  matrix products: 84.4 us -> 0 us
  blocking collectives: 0 us -> 77 us
  local copies, waits for them, and re-layouts: 72.6 us -> 2.82 us
  Pallas kernels: 0 us -> 57.2 us
  other arithmetic: 30.2 us -> 0.09 us
  starting transfers between devices: 0.81 us -> 29.8 us
  loops' own time: 15.4 us -> 0 us
  between operations: 15.6 us -> 1.5 us
    psum x6 -> x0, waiting for transfers between devices: 362 us -> none  [the longest x2 266 us: exit_waves(): lax.psum((probe_term_re, probe_term_im, probe_weight), ('tile', 'tm'))]
    reduce_scatter x2 -> x0, waiting for transfers between devices: 193 us -> none  [body(): lax.psum_scatter(accumulator, 'tm', scatter_dimension=2, tiled=True)]
    all_gather x2 -> x0, waiting for transfers between devices: 118 us -> none  [body(): band_tile = lax.all_gather(low_tile, 'tm', axis=2, tiled=True)]
    dot_general x24 -> x0, matrix products: 84.4 us -> none  [the longest x4 19.7 us: right_product(): jnp.einsum('...nm,mk->...nk', real_part + imag_part, mat_sum, precision=H...]
    all_to_all x0 -> x5, blocking collectives: none -> 77 us  [exchange(): return lax.all_to_all(x, 'tm', 0, 0)]
    pallas_call x0 -> x13, Pallas kernels: none -> 57.2 us  [the longest x2 45 us: body(): call(functools.partial(position_kernel, iteration > 0), (part, part, arr(...]
    dynamic_update_slice x4 -> x0, local copies, waits for them, and re-layouts: 35.1 us -> none  [deposit(): lax.dynamic_update_slice(accumulator, region + piece, (0, rows_at[slot_id...]
    ppermute x0 -> x12, starting transfers between devices: none -> 21 us  [the longest x6 14.6 us: swap(): return lax.ppermute(x, 'mode', SWAP)]
  transfers between devices with their start and end apart: 10 -> 13, of which waited for: 10 -> 10; matrix products, arithmetic and copies ran while one was open for 1% -> 0% of each run, Pallas kernels for 0% -> 4%
where the time goes in v1:
time: 190 us; the launch traced here: 189 us
  blocking collectives  77 us (41%)
  Pallas kernels  57.2 us (30%)
  starting transfers between devices  29.8 us (16%)
  waiting for transfers between devices  20.7 us (11%)
  local copies, waits for them, and re-layouts  2.82 us (1%)
    all_to_all x5, blocking collectives, exchange(): return lax.all_to_all(x, 'tm', 0, 0)  77 us
    pallas_call x2, Pallas kernels, body(): call(functools.partial(position_kernel, iteration > 0), (part, part, arr(...  45 us
    ppermute x6, starting transfers between devices, swap(): return lax.ppermute(x, 'mode', SWAP)  14.6 us
    ppermute x6, waiting for transfers between devices, swap(): return lax.ppermute(x, 'mode', SWAP)  9.4 us
    all_to_all x1, waiting for transfers between devices, exchange(): return lax.all_to_all(x, 'tm', 0, 0)  9.26 us
    all_to_all x1, starting transfers between devices, exchange(): return lax.all_to_all(x, 'tm', 0, 0)  8.73 us
    ppermute x6, starting transfers between devices, over_tiles(): lax.ppermute(x, 'tile', [(i, (i + k) % n) for i in range(n)])  6.48 us
  transfers between devices with their start and end apart: 13, of which 10 were waited for; matrix products, arithmetic and copies ran while one was open for 0% of the time, Pallas kernels for 4%

profile of v1, /device:TPU:1, one launch (start us, length us, event | category | flops | bytes accessed | tf_op | source)
XLA Modules:
  0.0 189.1 jit_solution(9355814940522091587)
XLA Ops:
  3.1 1.4 shard_map.122
  4.5 8.7 %all-to-all-start = ((f32[16,32,256]{2,1,0:T(8,128)}), f32[16,32,256]{2,1,0:T(8,128)S(1)}, u32[]{:S(2)}, u32[]{:S(2)}) async-start(f32[16,32,256]{2,1,0:T(8,128)} %shard_map.122), calls=%async_computation | async-start | bytes 1048576 | tf_op jit(solution)/shard_map/all_to_all | solution.py:359
  14.3 9.3 %all-to-all-done.obj = f32[16,32,256]{2,1,0:T(8,128)S(1)} async-done(((f32[16,32,256]{2,1,0:T(8,128)}), f32[16,32,256]{2,1,0:T(8,128)S(1)}, u32[]{:S(2)}, u32[]{:S(2)}) %all-to-all-start) | async-done | bytes 524320 | tf_op jit(solution)/shard_map/all_to_all | solution.py:359
  23.6 1.2 shard_map.123
  24.8 10.7 %all_to_all.30.h_own = bf16[16,32,256]{2,1,0:T(8,128)(2,1)S(1)} all-to-all(bf16[16,32,256]{2,1,0:T(8,128)(2,1)S(1)} %shard_map.123), channel_id=1, replica_groups=mesh['tile'=4,'tm'=16,'mode'=2] {'tm'}, dimensions={0} | all-to-all | bytes 524288 | tf_op jit(solution)/shard_map/all_to_all | solution.py:359
  35.5 3.2 %collective-permute-start.1 = (bf16[16,32,256]{2,1,0:T(8,128)(2,1)S(1)}, bf16[16,32,256]{2,1,0:T(8,128)(2,1)S(1)}, u32[]{:S(2)}, u32[]{:S(2)}) collective-permute-start(bf16[16,32,256]{2,1,0:T(8,128)(2,1)S(1)} %all_to_all.30.h_own), channel_id=1, source_target_pairs={{0,1},{1,0},{2,3},{3,2},{4,5},{5,4},{6,7},{7,6},{8,9},{9,8},{10,11... | collective-permute-start | bytes 786440 | tf_op jit(solution)/shard_map/ppermute | solution.py:362
  40.9 22.1 %shard_map.124 = (bf16[16,112,256]{2,1,0:T(8,128)(2,1)S(1)}, bf16[16,112,256]{2,1,0:T(8,128)(2,1)S(1)}, f32[272,256]{1,0:T(8,128)S(1)}) custom-call(s32[2]{0:T(128)S(1)} %pad_add_fusion.idx, s32[2]{0:T(128)S(1)} %copy-done.4, s32[2]{0:T(128)S(1)} %copy-done.5, s32[1]{0:T(128)S(6)} %copy.24.live_counts, bf16[512,512]{1,0:T(8,128)(2,1)S(1)} %copy-done.10, ...), custom_call_target="tpu_custom_call" | custom-call | flops 6442450944 | bytes 10485760 | tf_op jit(solution)/shard_map/pallas_call | solution.py:381
  63.5 2.1 %collective-permute-done.2.recv = bf16[16,112,256]{2,1,0:T(8,128)(2,1)S(1)} collective-permute-done((bf16[16,112,256]{2,1,0:T(8,128)(2,1)S(1)}, bf16[16,112,256]{2,1,0:T(8,128)(2,1)S(1)}, u32[]{:S(2)}, u32[]{:S(2)}) %collective-permute-start.2) | collective-permute-done | bytes 917536 | tf_op jit(solution)/shard_map/ppermute | solution.py:362
  66.4 19.2 %all_to_all.31.parts = bf16[16,128,256]{2,1,0:T(8,128)(2,1)S(1)} all-to-all(bf16[16,128,256]{2,1,0:T(8,128)(2,1)S(1)} %shard_map.125), channel_id=1, replica_groups=mesh['tile'=4,'tm'=16,'mode'=2] {'tm'}, dimensions={0} | all-to-all | bytes 2097152 | tf_op jit(solution)/shard_map/all_to_all | solution.py:359
  85.7 2.5 %collective-permute-start.5 = (bf16[80,256]{1,0:T(8,128)(2,1)S(1)}, bf16[80,256]{1,0:T(8,128)(2,1)S(1)}, u32[]{:S(2)}, u32[]{:S(2)}) collective-permute-start(bf16[80,256]{1,0:T(8,128)(2,1)S(1)} %shard_map.126.own), channel_id=1, source_target_pairs={{0,96},{32,0},{64,32},{96,64},{1,97},{33,1},{65,33},{97,65},{2,98}... | collective-permute-start | bytes 122888 | tf_op jit(solution)/shard_map/ppermute | solution.py:366
  89.4 3.0 %shard_map.127 = (bf16[16,32,256]{2,1,0:T(8,128)(2,1)S(1)}, f32[16,24,256]{2,1,0:T(8,128)S(1)}) custom-call(s32[16,8]{1,0:T(8,128)S(1)} %bitcast.4, s32[2]{0:T(128)S(1)} %pad_add_fusion.idx, bf16[16,128,256]{2,1,0:T(8,128)(2,1)S(1)} %all_to_all.31.parts, f32[272,256]{1,0:T(8,128)S(1)} %get-tuple-element.12.power, f32[16,32,256]{2,1,0:T(8,128)S(1)} %all-to-all-done.obj), custom_call_target="tpu_custom_call" | custom-call | bytes 8388608 | tf_op jit(solution)/shard_map/pallas_call | solution.py:409
  93.2 14.0 %all_to_all.32.h_own.h_one = bf16[16,96,256]{2,1,0:T(8,128)(2,1)S(1)} all-to-all(bf16[16,96,256]{2,1,0:T(8,128)(2,1)S(1)} %shard_map.128), channel_id=1, replica_groups=mesh['tile'=4,'tm'=16,'mode'=2] {'tm'}, dimensions={0} | all-to-all | bytes 1572864 | tf_op jit(solution)/shard_map/all_to_all | solution.py:359
  107.3 4.7 %collective-permute-start.6 = (bf16[16,96,256]{2,1,0:T(8,128)(2,1)S(1)}, bf16[16,96,256]{2,1,0:T(8,128)(2,1)S(1)}, u32[]{:S(2)}, u32[]{:S(2)}) collective-permute-start(bf16[16,96,256]{2,1,0:T(8,128)(2,1)S(1)} %all_to_all.32.h_own.h_one), channel_id=1, source_target_pairs={{0,1},{1,0},{2,3},{3,2},{4,5},{5,4},{6,7},{7,6},{8,9},{9,8},{10,11... | collective-permute-start | bytes 2359304 | tf_op jit(solution)/shard_map/ppermute | solution.py:362
  112.0 1.9 %collective-permute-done.6.h_oth = bf16[16,96,256]{2,1,0:T(8,128)(2,1)S(1)} collective-permute-done((bf16[16,96,256]{2,1,0:T(8,128)(2,1)S(1)}, bf16[16,96,256]{2,1,0:T(8,128)(2,1)S(1)}, u32[]{:S(2)}, u32[]{:S(2)}) %collective-permute-start.6) | collective-permute-done | bytes 786464 | tf_op jit(solution)/shard_map/ppermute | solution.py:362
  113.9 22.9 %shard_map.129 = (bf16[16,112,256]{2,1,0:T(8,128)(2,1)S(1)}, bf16[16,112,256]{2,1,0:T(8,128)(2,1)}, f32[272,256]{1,0:T(8,128)S(1)}) custom-call(s32[2]{0:T(128)S(1)} %pad_add_fusion.idx, s32[2]{0:T(128)S(1)} %copy-done.4, s32[2]{0:T(128)S(1)} %copy-done.5, s32[1]{0:T(128)S(6)} %copy.24.live_counts, bf16[512,512]{1,0:T(8,128)(2,1)S(1)} %copy-done.11, ...), custom_call_target="tpu_custom_call" | custom-call | flops 6442450944 | bytes 10485760 | tf_op jit(solution)/shard_map/pallas_call | solution.py:381
  137.1 2.3 %collective-permute-done.7.recv = bf16[16,112,256]{2,1,0:T(8,128)(2,1)S(1)} collective-permute-done((bf16[16,112,256]{2,1,0:T(8,128)(2,1)}, bf16[16,112,256]{2,1,0:T(8,128)(2,1)S(1)}, u32[]{:S(2)}, u32[]{:S(2)}) %collective-permute-start.7) | collective-permute-done | bytes 917536 | tf_op jit(solution)/shard_map/ppermute | solution.py:362
  140.3 19.1 %all_to_all.33.parts = bf16[16,128,256]{2,1,0:T(8,128)(2,1)S(1)} all-to-all(bf16[16,128,256]{2,1,0:T(8,128)(2,1)S(1)} %shard_map.130), channel_id=1, replica_groups=mesh['tile'=4,'tm'=16,'mode'=2] {'tm'}, dimensions={0} | all-to-all | bytes 2097152 | tf_op jit(solution)/shard_map/all_to_all | solution.py:359
  159.5 1.6 collective-permute-start.10
  161.1 1.2 collective-permute-start.9
  162.3 2.6 %shard_map.132.objs = bf16[16,32,256]{2,1,0:T(8,128)(2,1)S(1)} custom-call(s32[16,8]{1,0:T(8,128)S(1)} %bitcast.5, s32[2]{0:T(128)S(1)} %pad_add_fusion.idx, bf16[16,128,256]{2,1,0:T(8,128)(2,1)S(1)} %all_to_all.33.parts, f32[272,256]{1,0:T(8,128)S(1)} %get-tuple-element.16.power, f32[16,24,256]{2,1,0:T(8,128)S(1)} %get-tuple-element.17.upd), custom_call_target="tpu_custom_call" | custom-call | bytes 8388608 | tf_op jit(solution)/shard_map/pallas_call | solution.py:417
  166.5 14.0 %all_to_all.34.h_own = bf16[16,96,256]{2,1,0:T(8,128)(2,1)S(1)} all-to-all(bf16[16,96,256]{2,1,0:T(8,128)(2,1)S(1)} %shard_map.133), channel_id=1, replica_groups=mesh['tile'=4,'tm'=16,'mode'=2] {'tm'}, dimensions={0} | all-to-all | bytes 1572864 | tf_op jit(solution)/shard_map/all_to_all | solution.py:359
  180.6 4.7 %collective-permute-start.11 = (bf16[16,96,256]{2,1,0:T(8,128)(2,1)S(1)}, bf16[16,96,256]{2,1,0:T(8,128)(2,1)S(1)}, u32[]{:S(2)}, u32[]{:S(2)}) collective-permute-start(bf16[16,96,256]{2,1,0:T(8,128)(2,1)S(1)} %all_to_all.34.h_own), channel_id=1, source_target_pairs={{0,1},{1,0},{2,3},{3,2},{4,5},{5,4},{6,7},{7,6},{8,9},{9,8},{10,11... | collective-permute-start | bytes 2359304 | tf_op jit(solution)/shard_map/ppermute | solution.py:362
  185.3 1.9 %collective-permute-done.11.h_oth = bf16[16,96,256]{2,1,0:T(8,128)(2,1)S(1)} collective-permute-done((bf16[16,96,256]{2,1,0:T(8,128)(2,1)S(1)}, bf16[16,96,256]{2,1,0:T(8,128)(2,1)S(1)}, u32[]{:S(2)}, u32[]{:S(2)}) %collective-permute-start.11) | collective-permute-done | bytes 786464 | tf_op jit(solution)/shard_map/ppermute | solution.py:362
  187.2 1.9 %shard_map.134 = (f32[2,264,256]{2,1,0:T(8,128)}, f32[2,2,256,256]{3,2,1,0:T(8,128)}) custom-call(s32[2]{0:T(128)S(1)} %pad_add_fusion.idx, f32[2,264,256]{2,1,0:T(8,128)S(1)} %copy-done.1, f32[2,2,256,256]{3,2,1,0:T(8,128)S(1)} %copy-done.3, bf16[16,96,256]{2,1,0:T(8,128)(2,1)S(1)} %all_to_all.32.h_own.h_one, bf16[16,96,256]{2,1,0:T(8,128)(2,1)S(1)} %all_to_all.34.h_own, ...), custom_call_target="tpu_custom_call" | custom-call | bytes 1048576 | tf_op jit(solution)/shard_map/pallas_call | solution.py:429
  (49 shorter events, 11.3 us)
Async XLA Ops:
  0.6 0.7 copy-start.12
  2.1 1.0 copy-start
  3.1 10.1 %copy-start.2 = (f32[2,2,256,256]{3,2,1,0:T(8,128)S(1)}, f32[2,2,256,256]{3,2,1,0:T(8,128)}, u32[]{:S(2)}) copy-start(f32[2,2,256,256]{3,2,1,0:T(8,128)} %p_own.5) | copy-start | bytes 3145732
  4.5 35.4 %copy-start.8 = (bf16[512,512]{1,0:T(8,128)(2,1)S(1)}, bf16[512,512]{1,0:T(8,128)(2,1)}, u32[]{:S(2)}) copy-start(bf16[512,512]{1,0:T(8,128)(2,1)} %constant.18.clone.nh) | copy-start | bytes 1572868
  4.5 35.4 %copy-start.9 = (bf16[512,512]{1,0:T(8,128)(2,1)S(1)}, bf16[512,512]{1,0:T(8,128)(2,1)}, u32[]{:S(2)}) copy-start(bf16[512,512]{1,0:T(8,128)(2,1)} %constant.17.clone.ml) | copy-start | bytes 1572868
  4.5 19.0 %all-to-all-start = ((f32[16,32,256]{2,1,0:T(8,128)}), f32[16,32,256]{2,1,0:T(8,128)S(1)}, u32[]{:S(2)}, u32[]{:S(2)}) async-start(f32[16,32,256]{2,1,0:T(8,128)} %shard_map.122), calls=%async_computation | async-start | bytes 1048576 | tf_op jit(solution)/shard_map/all_to_all | solution.py:359
  13.3 26.6 %collective-permute-start = (f32[2,2,256,256]{3,2,1,0:T(8,128)S(1)}, f32[2,2,256,256]{3,2,1,0:T(8,128)}, u32[]{:S(2)}, u32[]{:S(2)}) collective-permute-start(f32[2,2,256,256]{3,2,1,0:T(8,128)S(1)} %copy-done.2), channel_id=1, source_target_pairs={{0,1},{1,0},{2,3},{3,2},{4,5},{5,4},{6,7},{7,6},{8,9},{9,8},{10,11... | collective-permute-start | bytes 3145736 | tf_op jit(solution)/shard_map/ppermute | solution.py:362
  23.6 16.3 %copy-start.6 = (f32[2,256,256]{2,1,0:T(8,128)S(1)}, f32[2,256,256]{2,1,0:T(8,128)}, u32[]{:S(2)}) copy-start(f32[2,256,256]{2,1,0:T(8,128)} %amp.3) | copy-start | bytes 1572868
  23.6 16.3 %copy-start.7 = (bf16[512,512]{1,0:T(8,128)(2,1)S(1)}, bf16[512,512]{1,0:T(8,128)(2,1)}, u32[]{:S(2)}) copy-start(bf16[512,512]{1,0:T(8,128)(2,1)} %constant.19.clone.nl) | copy-start | bytes 1572868
  35.5 4.4 %collective-permute-start.1 = (bf16[16,32,256]{2,1,0:T(8,128)(2,1)S(1)}, bf16[16,32,256]{2,1,0:T(8,128)(2,1)S(1)}, u32[]{:S(2)}, u32[]{:S(2)}) collective-permute-start(bf16[16,32,256]{2,1,0:T(8,128)(2,1)S(1)} %all_to_all.30.h_own), channel_id=1, source_target_pairs={{0,1},{1,0},{2,3},{3,2},{4,5},{5,4},{6,7},{7,6},{8,9},{9,8},{10,11... | collective-permute-start | bytes 786440 | tf_op jit(solution)/shard_map/ppermute | solution.py:362
  39.9 1.0 copy-start.10
  63.0 2.6 %collective-permute-start.2 = (bf16[16,112,256]{2,1,0:T(8,128)(2,1)S(1)}, bf16[16,112,256]{2,1,0:T(8,128)(2,1)S(1)}, u32[]{:S(2)}, u32[]{:S(2)}) collective-permute-start(bf16[16,112,256]{2,1,0:T(8,128)(2,1)S(1)} %get-tuple-element.11), channel_id=1, source_target_pairs={{0,1},{1,0},{2,3},{3,2},{4,5},{5,4},{6,7},{7,6},{8,9},{9,8},{10,11... | collective-permute-start | bytes 2752520 | tf_op jit(solution)/shard_map/ppermute | solution.py:362
  85.7 6.7 %collective-permute-start.5 = (bf16[80,256]{1,0:T(8,128)(2,1)S(1)}, bf16[80,256]{1,0:T(8,128)(2,1)S(1)}, u32[]{:S(2)}, u32[]{:S(2)}) collective-permute-start(bf16[80,256]{1,0:T(8,128)(2,1)S(1)} %shard_map.126.own), channel_id=1, source_target_pairs={{0,96},{32,0},{64,32},{96,64},{1,97},{33,1},{65,33},{97,65},{2,98}... | collective-permute-start | bytes 122888 | tf_op jit(solution)/shard_map/ppermute | solution.py:366
  88.3 4.4 %collective-permute-start.4 = (bf16[80,256]{1,0:T(8,128)(2,1)S(1)}, bf16[80,256]{1,0:T(8,128)(2,1)S(1)}, u32[]{:S(2)}, u32[]{:S(2)}) collective-permute-start(bf16[80,256]{1,0:T(8,128)(2,1)S(1)} %shard_map.126.own), channel_id=1, source_target_pairs={{0,64},{32,96},{64,0},{96,32},{1,65},{33,97},{65,1},{97,33},{2,66}... | collective-permute-start | bytes 122888 | tf_op jit(solution)/shard_map/ppermute | solution.py:366
  88.8 4.3 %collective-permute-start.3 = (bf16[80,256]{1,0:T(8,128)(2,1)S(1)}, bf16[80,256]{1,0:T(8,128)(2,1)S(1)}, u32[]{:S(2)}, u32[]{:S(2)}) collective-permute-start(bf16[80,256]{1,0:T(8,128)(2,1)S(1)} %shard_map.126.own), channel_id=1, source_target_pairs={{0,32},{32,64},{64,96},{96,0},{1,33},{33,65},{65,97},{97,1},{2,34}... | collective-permute-start | bytes 122888 | tf_op jit(solution)/shard_map/ppermute | solution.py:366
  93.2 20.7 %copy-start.11 = (bf16[512,512]{1,0:T(8,128)(2,1)S(1)}, bf16[512,512]{1,0:T(8,128)(2,1)}, u32[]{:S(2)}) copy-start(bf16[512,512]{1,0:T(8,128)(2,1)} %constant.16.clone.mh) | copy-start | bytes 1572868
  107.3 6.6 %collective-permute-start.6 = (bf16[16,96,256]{2,1,0:T(8,128)(2,1)S(1)}, bf16[16,96,256]{2,1,0:T(8,128)(2,1)S(1)}, u32[]{:S(2)}, u32[]{:S(2)}) collective-permute-start(bf16[16,96,256]{2,1,0:T(8,128)(2,1)S(1)} %all_to_all.32.h_own.h_one), channel_id=1, source_target_pairs={{0,1},{1,0},{2,3},{3,2},{4,5},{5,4},{6,7},{7,6},{8,9},{9,8},{10,11... | collective-permute-start | bytes 2359304 | tf_op jit(solution)/shard_map/ppermute | solution.py:362
  136.8 2.7 %collective-permute-start.7 = (bf16[16,112,256]{2,1,0:T(8,128)(2,1)}, bf16[16,112,256]{2,1,0:T(8,128)(2,1)S(1)}, u32[]{:S(2)}, u32[]{:S(2)}) collective-permute-start(bf16[16,112,256]{2,1,0:T(8,128)(2,1)} %get-tuple-element.15), channel_id=1, source_target_pairs={{0,1},{1,0},{2,3},{3,2},{4,5},{5,4},{6,7},{7,6},{8,9},{9,8},{10,11... | collective-permute-start | bytes 2752520 | tf_op jit(solution)/shard_map/ppermute | solution.py:362
  159.5 5.4 %collective-permute-start.10 = (bf16[80,256]{1,0:T(8,128)(2,1)S(1)}, bf16[80,256]{1,0:T(8,128)(2,1)S(1)}, u32[]{:S(2)}, u32[]{:S(2)}) collective-permute-start(bf16[80,256]{1,0:T(8,128)(2,1)S(1)} %shard_map.131.own), channel_id=1, source_target_pairs={{0,96},{32,0},{64,32},{96,64},{1,97},{33,1},{65,33},{97,65},{2,98}... | collective-permute-start | bytes 122888 | tf_op jit(solution)/shard_map/ppermute | solution.py:366
  161.1 4.4 %collective-permute-start.9 = (bf16[80,256]{1,0:T(8,128)(2,1)S(1)}, bf16[80,256]{1,0:T(8,128)(2,1)S(1)}, u32[]{:S(2)}, u32[]{:S(2)}) collective-permute-start(bf16[80,256]{1,0:T(8,128)(2,1)S(1)} %shard_map.131.own), channel_id=1, source_target_pairs={{0,64},{32,96},{64,0},{96,32},{1,65},{33,97},{65,1},{97,33},{2,66}... | collective-permute-start | bytes 122888 | tf_op jit(solution)/shard_map/ppermute | solution.py:366
  162.3 4.1 %collective-permute-start.8 = (bf16[80,256]{1,0:T(8,128)(2,1)S(1)}, bf16[80,256]{1,0:T(8,128)(2,1)S(1)}, u32[]{:S(2)}, u32[]{:S(2)}) collective-permute-start(bf16[80,256]{1,0:T(8,128)(2,1)S(1)} %shard_map.131.own), channel_id=1, source_target_pairs={{0,32},{32,64},{64,96},{96,0},{1,33},{33,65},{65,97},{97,1},{2,34}... | collective-permute-start | bytes 122888 | tf_op jit(solution)/shard_map/ppermute | solution.py:366
  166.4 20.8 %copy-start.3 = (f32[2,2,256,256]{3,2,1,0:T(8,128)S(1)}, f32[2,2,256,256]{3,2,1,0:T(8,128)}, u32[]{:S(2)}) copy-start(f32[2,2,256,256]{3,2,1,0:T(8,128)} %p_own.5) | copy-start | bytes 3145732
  166.5 20.7 %copy-start.1 = (f32[2,264,256]{2,1,0:T(8,128)S(1)}, f32[2,264,256]{2,1,0:T(8,128)}, u32[]{:S(2)}) copy-start(f32[2,264,256]{2,1,0:T(8,128)} %obj.3) | copy-start | bytes 1622020
  180.6 6.6 %collective-permute-start.11 = (bf16[16,96,256]{2,1,0:T(8,128)(2,1)S(1)}, bf16[16,96,256]{2,1,0:T(8,128)(2,1)S(1)}, u32[]{:S(2)}, u32[]{:S(2)}) collective-permute-start(bf16[16,96,256]{2,1,0:T(8,128)(2,1)S(1)} %all_to_all.34.h_own), channel_id=1, source_target_pairs={{0,1},{1,0},{2,3},{3,2},{4,5},{5,4},{6,7},{7,6},{8,9},{9,8},{10,11... | collective-permute-start | bytes 2359304 | tf_op jit(solution)/shard_map/ppermute | solution.py:362
  (2 other events, 1.3 us)
